TPU v7x, 128 devices: a whole 4x4x4 slice. The times are simulated.
128 devices in a mesh: energy: 8 (over z, core), views: 16 (over y, x).
Axes of the slice: x: 4, y: 4, z: 4, core: 2. Of those that a mesh axis runs over, the one named last changes fastest.
Arguments:
- projector_tiles: float32 [64, 48, 128, 256], P('views'), may hold values from -0.0546875 to 0.0546875
- tile_blocks: int32 [64, 48], P('views'), may hold values from 0 to 255
- ray_counts: int32 [64], P('views'), may hold values from 64 to 128
- sinogram: float32 [64, 8192], P('energy', 'views'), may hold values from -6 to 6
- ray_weights: float32 [64, 8192], P('energy', 'views'), may hold values from 0.25 to 4
- start_volume: float32 [64, 65536], P('energy', 'views'), may hold values from -6 to 6
- split_target: float32 [16, 64, 4096], P('views', None, 'energy'), may hold values from -6 to 6
- scaled_dual: float32 [16, 64, 4096], P('views', None, 'energy'), may hold values from -3 to 3
Outputs:
- new_volume: float32 [64, 65536], P('energy', 'views')
- new_split: float32 [16, 64, 4096], P('views', None, 'energy')
- new_dual: float32 [16, 64, 4096], P('views', None, 'energy')
Inputs may be any that keep to these rules, and one draw needn't show every extreme that they name: `tile_blocks`: block indices may repeat within a ray block. `ray_counts`: rays of a block at or past its count are padding.
All inputs are finite; a program needn't handle non-finite values.
Results may differ from a plain program's by a relative error of at most 0.00022.
Values sent between devices are 32-bit elements; how exact they have to be, the bound alone decides.
A program may use at most 128 MiB of HBM per device.

v0:
```python
import jax
import jax.numpy as jnp
from jax import lax
from jax.sharding import PartitionSpec as P

PV = 64
ITERS = 3
PENALTY = 1.0
SHRINK = 16.0
exact_mode = lax.Precision.HIGHEST


def forward(gathered, projector_tiles, tile_blocks):
    channel_count = gathered.shape[0]
    block_voxels = projector_tiles.shape[3]
    block_grid = gathered.reshape(channel_count, -1, block_voxels)
    columns = block_grid[:, tile_blocks]
    projected = jnp.einsum("crtv,rtkv->crk", columns, projector_tiles, precision=exact_mode)
    return projected.reshape(channel_count, -1)


def backward(weighted, projector_tiles, tile_blocks, voxel_count):
    channel_count = weighted.shape[0]
    ray_blocks, per_block, ray_length, block_voxels = projector_tiles.shape
    ray_parts = weighted.reshape(channel_count, ray_blocks, ray_length)
    spread_rays = jnp.einsum("crk,rtkv->crtv", ray_parts, projector_tiles, precision=exact_mode)
    block_grid = jnp.zeros((channel_count, voxel_count // block_voxels, block_voxels), jnp.float32)
    block_grid = block_grid.at[:, tile_blocks.reshape(-1)].add(
        spread_rays.reshape(channel_count, ray_blocks * per_block, block_voxels)
    )
    return block_grid.reshape(channel_count, voxel_count)


def shrink_patches(merged):
    leading, channel_count, segment_len = merged.shape
    blocks = merged.reshape(channel_count, segment_len // PV, PV)
    gram_matrix = jnp.einsum("cpv,dpv->pcd", blocks, blocks, precision=exact_mode)
    shifted = gram_matrix + SHRINK * jnp.eye(channel_count, dtype=jnp.float32)
    factor = jnp.linalg.cholesky(shifted)
    right_side = jnp.transpose(blocks, (1, 0, 2))
    solved = jax.scipy.linalg.cho_solve((factor, True), right_side)
    shrunk = right_side - SHRINK * solved
    return jnp.transpose(shrunk, (1, 0, 2)).reshape(leading, channel_count, segment_len)


def local(
    projector_tiles,
    tile_blocks,
    ray_counts,
    sinogram,
    ray_weights,
    start_volume,
    split_target,
    scaled_dual,
):
    ray_length = projector_tiles.shape[2]
    live_rays = (
        lax.broadcasted_iota(jnp.int32, (ray_counts.shape[0], ray_length), 1) < ray_counts[:, None]
    ).astype(jnp.float32)
    ray_scale = ray_weights * live_rays.reshape(1, -1)
    target_shard = lax.all_to_all(
        split_target - scaled_dual, "energy", split_axis=1, concat_axis=2, tiled=True
    )[0]
    segment = target_shard.shape[1]
    voxel_count = segment * lax.axis_size("views")
    volume_now, target = (start_volume, target_shard)

    def normal_map(vector, measured, anchor):
        gathered = lax.all_gather(vector, "views", axis=1, tiled=True)
        weighted = ray_scale * (measured - forward(gathered, projector_tiles, tile_blocks))
        partial_sum = backward(weighted, projector_tiles, tile_blocks, voxel_count)
        summed = lax.psum_scatter(partial_sum, "views", scatter_dimension=1, tiled=True)
        return summed + PENALTY * (anchor - vector)

    residual = normal_map(volume_now, sinogram, target)

    def norm_total(vector):
        return lax.psum(jnp.sum(jnp.square(vector), axis=1), "views")

    direction = residual
    norm_now = norm_total(residual)
    for iteration in range(ITERS):
        mapped = -normal_map(direction, 0.0, 0.0)
        curvature = lax.psum(jnp.sum(direction * mapped, axis=1), "views")
        step_size = (norm_now / curvature)[:, None]
        volume_now = volume_now + step_size * direction
        if iteration + 1 < ITERS:
            residual = residual - step_size * mapped
            norm_next = norm_total(residual)
            direction = residual + (norm_next / norm_now)[:, None] * direction
            norm_now = norm_next
    volume_patch = lax.all_to_all(
        volume_now[None], "energy", split_axis=2, concat_axis=1, tiled=True
    )
    new_split = shrink_patches(volume_patch + scaled_dual)
    new_dual = scaled_dual + volume_patch - new_split
    return (volume_now, new_split, new_dual)


def solution(mesh):
    placed = (
        P("views", None, None, None),
        P("views", None),
        P("views"),
        P("energy", "views"),
        P("energy", "views"),
        P("energy", "views"),
        P("views", None, "energy"),
        P("views", None, "energy"),
    )
    return jax.shard_map(
        local,
        mesh=mesh,
        in_specs=placed,
        out_specs=(P("energy", "views"), P("views", None, "energy"), P("views", None, "energy")),
        check_vma=False,
    )
```

profile of v0, /device:TPU:1, one launch (start us, length us, event | category | flops | bytes accessed | tf_op | source)
XLA Modules:
  0.0 1047.2 jit_solution(1356048474511867620)
XLA Ops:
  10.2 47.1 %all-gather.5.cloned.1.call-done = f32[8,65536]{1,0:T(8,128)} async-done(((f32[8,4096]{1,0:T(8,128)}), f32[8,65536]{1,0:T(8,128)}) %all-gather.5.cloned.1.call-update) | async-done | bytes 2097168 | tf_op jit(solution)/shard_map/all_gather | solution.py:69
  59.7 24.1 %fusion.16 = f32[8,4,128,1]{2,0,3,1:T(8,128)S(1)} fusion(f32[8,512]{1,0:T(8,128)S(1)} %copy-done.14, f32[8,4,48,256]{3,0,2,1:T(8,128)S(1)} %bitcast.197, f32[4,48,128,256]{3,2,1,0:T(8,128)} %param.8, f32[8,512]{1,0:T(8,128)S(1)} %copy-done.12, f32[512]{0:T(512)S(1)} %convert_bitcast_fusion), kind=kOutput, calls=%fused_computation.29 | convolution fusion | flops 603992064 | bytes 26789888 | tf_op jit(solution)/shard_map/crtv,rtkv->crk/dot_general | solution.py:18
  83.8 12.9 %fusion.26 = f32[4,8,48,256]{3,1,2,0:T(8,128)} fusion(f32[8,4,128,1]{2,0,3,1:T(8,128)S(1)} %fusion.16, f32[4,48,128,256]{3,2,1,0:T(8,128)S(1)} %copy-done), kind=kOutput, calls=%fused_computation.67 | convolution fusion | flops 603979776 | bytes 26755072 | tf_op jit(solution)/shard_map/crk,rtkv->crtv/dot_general | solution.py:26
  96.9 15.5 %scatter_fusion = f32[8,256,256]{2,0,1:T(8,128)S(1)} fusion(f32[8,256,256]{2,0,1:T(8,128)S(1)} %broadcast.144.clone, s32[192]{0:T(256)S(1)} %bitcast.206, f32[192,8,256]{2,1,0:T(8,128)} %bitcast.191), kind=kCustom, calls=%fused_computation.4 | custom fusion | flops 393216 | bytes 4719360 | tf_op jit(solution)/shard_map/scatter-add | solution.py:28
  114.0 11.0 %all_to_all.33 = f32[1,64,512]{2,0,1:T(1,128)S(1)} all-to-all(f32[1,64,512]{2,0,1:T(1,128)S(1)} %copy.60), channel_id=1, replica_groups=mesh['energy'=8,'views'=16] {'energy'}, dimensions={1} | all-to-all | bytes 262144 | tf_op jit(solution)/shard_map/all_to_all | solution.py:61
  125.0 61.7 %reduce-scatter.5.cloned.1.call-done = f32[8,4096]{1,0:T(8,128)} async-done(((f32[8,65536]{1,0:T(8,128)}), f32[8,4096]{1,0:T(8,128)}) %reduce-scatter.5.cloned.1.call-update) | async-done | bytes 131088 | tf_op jit(solution)/shard_map/reduce_scatter | solution.py:72
  188.6 46.1 %all-gather.7.cloned.1.call-done = f32[8,65536]{1,0:T(8,128)} async-done(((f32[8,4096]{1,0:T(8,128)}), f32[8,65536]{1,0:T(8,128)}) %all-gather.7.cloned.1.call-update) | async-done | bytes 2097168 | tf_op jit(solution)/shard_map/all_gather | solution.py:69
  236.9 22.7 %fusion.13 = f32[8,4,128,1]{2,0,3,1:T(8,128)S(1)} fusion(f32[8,4,48,256]{3,0,2,1:T(8,128)S(1)} %bitcast.195, f32[4,48,128,256]{3,2,1,0:T(8,128)} %param.8, f32[8,512]{1,0:T(8,128)S(1)} %copy-done.12, f32[512]{0:T(512)S(1)} %convert_bitcast_fusion), kind=kOutput, calls=%fused_computation.25 | convolution fusion | flops 603992064 | bytes 26773504 | tf_op jit(solution)/shard_map/crtv,rtkv->crk/dot_general | solution.py:18
  259.6 15.8 %fusion.27 = f32[4,8,48,256]{3,1,2,0:T(8,128)} fusion(f32[8,4,128,1]{2,0,3,1:T(8,128)S(1)} %fusion.13, f32[4,48,128,256]{3,2,1,0:T(8,128)} %param.8), kind=kOutput, calls=%fused_computation.68 | convolution fusion | flops 603979776 | bytes 26755072 | tf_op jit(solution)/shard_map/crk,rtkv->crtv/dot_general | solution.py:26
  275.5 15.5 %scatter_fusion.1 = f32[8,256,256]{2,0,1:T(8,128)S(1)} fusion(f32[8,256,256]{2,0,1:T(8,128)S(1)} %broadcast.144.clone.1, s32[192]{0:T(256)S(1)} %bitcast.207, f32[192,8,256]{2,1,0:T(8,128)} %bitcast.192), kind=kCustom, calls=%fused_computation.5 | custom fusion | flops 393216 | bytes 4719360 | tf_op jit(solution)/shard_map/scatter-add | solution.py:28
  292.4 72.9 %reduce-scatter.7.cloned.1.call-done = f32[8,4096]{1,0:T(8,128)} async-done(((f32[8,65536]{1,0:T(8,128)}), f32[8,4096]{1,0:T(8,128)}) %reduce-scatter.7.cloned.1.call-update) | async-done | bytes 131088 | tf_op jit(solution)/shard_map/reduce_scatter | solution.py:72
  366.4 30.9 %all-reduce = (f32[8]{0:T(128)S(1)}, f32[8]{0:T(128)S(1)}) all-reduce(f32[8]{0:T(128)S(1)} %get-tuple-element.7, f32[8]{0:T(128)S(1)} %get-tuple-element.6), channel_id=1, replica_groups=mesh['energy'=8,'views'=16] {'views'}, use_global_device_ids=true, to_apply=%region_3.0 | all-reduce | flops 16 | bytes 128 | tf_op jit(solution)/shard_map/psum | solution.py:78
  398.4 28.5 %psum.44 = f32[8]{0:T(128)S(1)} all-reduce(f32[8]{0:T(128)S(1)} %get-tuple-element.10), channel_id=1, replica_groups=mesh['energy'=8,'views'=16] {'views'}, use_global_device_ids=true, to_apply=%region_9.0 | all-reduce | flops 8 | bytes 64 | tf_op jit(solution)/shard_map/psum | solution.py:78
  428.0 57.6 %all-gather.9.cloned.1.call-done = f32[8,65536]{1,0:T(8,128)} async-done(((f32[8,4096]{1,0:T(8,128)}), f32[8,65536]{1,0:T(8,128)}) %all-gather.9.cloned.1.call-update) | async-done | bytes 2097168 | tf_op jit(solution)/shard_map/all_gather | solution.py:69
  487.8 22.7 %fusion.9 = f32[8,4,128,1]{2,0,3,1:T(8,128)S(1)} fusion(f32[8,4,48,256]{3,0,2,1:T(8,128)S(1)} %bitcast.196, f32[4,48,128,256]{3,2,1,0:T(8,128)} %param.8, f32[8,512]{1,0:T(8,128)S(1)} %copy-done.12, f32[512]{0:T(512)S(1)} %convert_bitcast_fusion), kind=kOutput, calls=%fused_computation.20 | convolution fusion | flops 603992064 | bytes 26773504 | tf_op jit(solution)/shard_map/crtv,rtkv->crk/dot_general | solution.py:18
  510.5 15.8 %fusion.28 = f32[4,8,48,256]{3,1,2,0:T(8,128)} fusion(f32[8,4,128,1]{2,0,3,1:T(8,128)S(1)} %fusion.9, f32[4,48,128,256]{3,2,1,0:T(8,128)} %param.8), kind=kOutput, calls=%fused_computation.69 | convolution fusion | flops 603979776 | bytes 26755072 | tf_op jit(solution)/shard_map/crk,rtkv->crtv/dot_general | solution.py:26
  526.4 15.5 %scatter_fusion.2 = f32[8,256,256]{2,0,1:T(8,128)S(1)} fusion(f32[8,256,256]{2,0,1:T(8,128)S(1)} %broadcast.144.clone.2, s32[192]{0:T(256)S(1)} %bitcast.208, f32[192,8,256]{2,1,0:T(8,128)} %bitcast.193), kind=kCustom, calls=%fused_computation.6 | custom fusion | flops 393216 | bytes 4719360 | tf_op jit(solution)/shard_map/scatter-add | solution.py:28
  543.3 72.9 %reduce-scatter.9.cloned.1.call-done = f32[8,4096]{1,0:T(8,128)} async-done(((f32[8,65536]{1,0:T(8,128)}), f32[8,4096]{1,0:T(8,128)}) %reduce-scatter.9.cloned.1.call-update) | async-done | bytes 131088 | tf_op jit(solution)/shard_map/reduce_scatter | solution.py:72
  617.3 30.9 %psum.45 = f32[8]{0:T(128)S(1)} all-reduce(f32[8]{0:T(128)S(1)} %multiply_reduce_fusion.2), channel_id=1, replica_groups=mesh['energy'=8,'views'=16] {'views'}, use_global_device_ids=true, to_apply=%region_13.0 | all-reduce | flops 8 | bytes 64 | tf_op jit(solution)/shard_map/psum | solution.py:84
  649.3 28.5 %psum.46 = f32[8]{0:T(128)S(1)} all-reduce(f32[8]{0:T(128)S(1)} %multiply_reduce_fusion.1), channel_id=1, replica_groups=mesh['energy'=8,'views'=16] {'views'}, use_global_device_ids=true, to_apply=%region_15.0 | all-reduce | flops 8 | bytes 64 | tf_op jit(solution)/shard_map/psum | solution.py:78
  679.8 57.5 %all-gather.11.cloned.1.call-done = f32[8,65536]{1,0:T(8,128)} async-done(((f32[8,4096]{1,0:T(8,128)}), f32[8,65536]{1,0:T(8,128)}) %all-gather.11.cloned.1.call-update) | async-done | bytes 2097168 | tf_op jit(solution)/shard_map/all_gather | solution.py:69
  739.6 22.7 %fusion.5 = f32[8,4,128,1]{2,0,3,1:T(8,128)S(1)} fusion(f32[8,4,48,256]{3,0,2,1:T(8,128)S(1)} %bitcast.194, f32[4,48,128,256]{3,2,1,0:T(8,128)} %param.8, f32[8,512]{1,0:T(8,128)S(1)} %copy-done.12, f32[512]{0:T(512)S(1)} %convert_bitcast_fusion), kind=kOutput, calls=%fused_computation.15 | convolution fusion | flops 603992064 | bytes 26773504 | tf_op jit(solution)/shard_map/crtv,rtkv->crk/dot_general | solution.py:18
  762.3 15.8 %fusion.29 = f32[4,8,48,256]{3,1,2,0:T(8,128)} fusion(f32[8,4,128,1]{2,0,3,1:T(8,128)S(1)} %fusion.5, f32[4,48,128,256]{3,2,1,0:T(8,128)} %param.8), kind=kOutput, calls=%fused_computation.70 | convolution fusion | flops 603979776 | bytes 26755072 | tf_op jit(solution)/shard_map/crk,rtkv->crtv/dot_general | solution.py:26
  778.2 15.5 %scatter_fusion.3 = f32[8,256,256]{2,0,1:T(8,128)S(1)} fusion(f32[8,256,256]{2,0,1:T(8,128)S(1)} %broadcast.144, s32[192]{0:T(256)S(1)} %bitcast.209, f32[192,8,256]{2,1,0:T(8,128)} %bitcast.190), kind=kCustom, calls=%fused_computation.7 | custom fusion | flops 393216 | bytes 4719360 | tf_op jit(solution)/shard_map/scatter-add | solution.py:28
  795.1 73.0 %reduce-scatter.11.cloned.1.call-done = f32[8,4096]{1,0:T(8,128)} async-done(((f32[8,65536]{1,0:T(8,128)}), f32[8,4096]{1,0:T(8,128)}) %reduce-scatter.11.cloned.1.call-update) | async-done | bytes 131088 | tf_op jit(solution)/shard_map/reduce_scatter | solution.py:72
  869.1 31.3 %psum.47 = f32[8]{0:T(128)S(1)} all-reduce(f32[8]{0:T(128)S(1)} %multiply_reduce_fusion), channel_id=1, replica_groups=mesh['energy'=8,'views'=16] {'views'}, use_global_device_ids=true, to_apply=%region_19.0 | all-reduce | flops 8 | bytes 64 | tf_op jit(solution)/shard_map/psum | solution.py:84
  903.6 19.4 %reduce.6 = f32[4096,8]{1,0:T(8,128)} reduce(f32[4096,1,8]{2,1,0:T(1,128)S(1)} %bitcast.188, f32[]{:T(128)} %broadcast.181), dimensions={1}, to_apply=%bitcast.165.reduce_sub_computation | reduce | bytes 262148
  926.3 14.2 %all-to-all-start.1 = ((f32[8,1,4096]{2,1,0:T(1,128)}), f32[8,1,4096]{2,1,0:T(1,128)S(1)}, u32[]{:S(2)}, u32[]{:S(2)}) async-start(f32[8,1,4096]{2,1,0:T(1,128)} %reshape.254), calls=%async_computation.5 | async-start | bytes 262144 | tf_op jit(solution)/shard_map/all_to_all | solution.py:92
  940.5 5.2 all-to-all-done.1
  946.7 3.5 reshape.255
  951.6 46.9 %custom-call.11 = f32[8,64,64]{2,1,0:T(8,128)S(1)} custom-call(f32[8,64,64]{2,1,0:T(8,128)S(1)} %fusion.21), custom_call_target="Cholesky" | custom-call | tf_op jit(solution)/shard_map/jit(cholesky)/cholesky | solution.py:39
  998.8 39.3 %custom-call.12 = f32[8,1,64,64]{2,3,1,0:T(8,128)S(1)} custom-call(f32[8,1,64,64]{3,2,1,0:T(8,128)S(1)} %select_bitcast_fusion), custom_call_target="InvertDiagBlocksLowerTriangular" | custom-call | tf_op jit(solution)/shard_map/jit(_cho_solve)/vmap()/triangular_solve | solution.py:41
  (98 shorter events, 39.8 us)
Async XLA Ops:
  7.2 52.5 %copy-start.14 = (f32[8,512]{1,0:T(8,128)S(1)}, f32[8,512]{1,0:T(8,128)}, u32[]{:S(2)}) copy-start(f32[8,512]{1,0:T(8,128)} %param.11) | copy-start | bytes 49156
  7.2 52.5 %copy-start.12 = (f32[8,512]{1,0:T(8,128)S(1)}, f32[8,512]{1,0:T(8,128)}, u32[]{:S(2)}) copy-start(f32[8,512]{1,0:T(8,128)} %param.12) | copy-start | bytes 49156
  7.2 50.2 %all-gather.5.cloned.1.call-start = ((), (), s32[]{:S(2)}) async-start(), calls=%async_computation.6 | async-start | bytes 2228224 | tf_op jit(solution)/shard_map/all_gather | solution.py:69
  7.9 178.8 %reduce-scatter.5.cloned.1.call-start = ((), (), s32[]{:S(2)}) async-start(), calls=%async_computation.7 | async-start | bytes 2228224 | tf_op jit(solution)/shard_map/reduce_scatter | solution.py:72
  59.7 24.2 %copy-start = (f32[4,48,128,256]{3,2,1,0:T(8,128)S(1)}, f32[4,48,128,256]{3,2,1,0:T(8,128)}, u32[]{:S(2)}) copy-start(f32[4,48,128,256]{3,2,1,0:T(8,128)} %param.8) | copy-start | bytes 75497472
  112.4 1.4 copy-start.2
  112.4 1.4 copy-start.9
  112.4 1.4 copy-start.13
  112.4 74.3 %copy-start.8 = (f32[8,4096]{1,0:T(8,128)S(1)}, f32[8,4096]{1,0:T(8,128)}, u32[]{:S(2)}) copy-start(f32[8,4096]{1,0:T(8,128)} %param.13) | copy-start | bytes 393220
  113.8 120.9 %all-gather.7.cloned.1.call-start = ((), (), s32[]{:S(2)}) async-start(), calls=%async_computation.8 | async-start | bytes 2228224 | tf_op jit(solution)/shard_map/all_gather | solution.py:69
  188.3 177.0 %reduce-scatter.7.cloned.1.call-start = ((), (), s32[]{:S(2)}) async-start(), calls=%async_computation.9 | async-start | bytes 2228224 | tf_op jit(solution)/shard_map/reduce_scatter | solution.py:72
  291.0 1.4 copy-start.3
  291.0 74.3 %copy-start.5 = (f32[8,4096]{1,0:T(8,128)S(1)}, f32[8,4096]{1,0:T(8,128)}, u32[]{:S(2)}) copy-start(f32[8,4096]{1,0:T(8,128)} %subtract_add_fusion) | copy-start | bytes 393220
  292.4 193.2 %all-gather.9.cloned.1.call-start = ((), (), s32[]{:S(2)}) async-start(), calls=%async_computation.10 | async-start | bytes 2228224 | tf_op jit(solution)/shard_map/all_gather | solution.py:69
  427.7 188.5 %reduce-scatter.9.cloned.1.call-start = ((), (), s32[]{:S(2)}) async-start(), calls=%async_computation.11 | async-start | bytes 2228224 | tf_op jit(solution)/shard_map/reduce_scatter | solution.py:72
  541.9 1.4 copy-start.4
  541.9 74.3 %copy-start.6 = (f32[8,4096]{1,0:T(8,128)S(1)}, f32[8,4096]{1,0:T(8,128)}, u32[]{:S(2)}) copy-start(f32[8,4096]{1,0:T(8,128)} %multiply_add_fusion.2) | copy-start | bytes 393220
  543.3 194.0 %all-gather.11.cloned.1.call-start = ((), (), s32[]{:S(2)}) async-start(), calls=%async_computation.12 | async-start | bytes 2228224 | tf_op jit(solution)/shard_map/all_gather | solution.py:69
  679.5 188.5 %reduce-scatter.11.cloned.1.call-start = ((), (), s32[]{:S(2)}) async-start(), calls=%async_computation.13 | async-start | bytes 2228224 | tf_op jit(solution)/shard_map/reduce_scatter | solution.py:72
  793.7 1.4 copy-start.1
  793.7 74.3 %copy-start.7 = (f32[8,4096]{1,0:T(8,128)S(1)}, f32[8,4096]{1,0:T(8,128)}, u32[]{:S(2)}) copy-start(f32[8,4096]{1,0:T(8,128)} %multiply_add_fusion.1) | copy-start | bytes 393220
  900.6 22.4 %copy-start.11 = (f32[8,4096]{1,0:T(8,128)}, f32[8,4096]{1,0:T(8,128)S(1)}, u32[]{:S(2)}) copy-start(f32[8,4096]{1,0:T(8,128)S(1)} %multiply_add_fusion) | copy-start | bytes 393220
  926.3 19.4 %all-to-all-start.1 = ((f32[8,1,4096]{2,1,0:T(1,128)}), f32[8,1,4096]{2,1,0:T(1,128)S(1)}, u32[]{:S(2)}, u32[]{:S(2)}) async-start(f32[8,1,4096]{2,1,0:T(1,128)} %reshape.254), calls=%async_computation.5 | async-start | bytes 262144 | tf_op jit(solution)/shard_map/all_to_all | solution.py:92
  1039.4 0.7 copy-start.10
Sparse Core Ops, SparseCore 0:
  10.2 47.1 all-gather.4
  113.9 72.7 reduce-scatter.4
  189.7 44.9 all-gather.6
  292.5 72.7 reduce-scatter.6
  427.8 57.6 all-gather.8
  543.4 72.7 reduce-scatter.8
  679.6 57.6 all-gather.10
  795.2 72.7 reduce-scatter.10
where the time goes:
time: 1060 us; the launch traced here: 1050 us
  waiting for transfers between devices  495 us (47%)
  other arithmetic  180 us (17%)
  blocking collectives  161 us (15%)
  matrix products  154 us (15%)
  local copies, waits for them, and re-layouts  27 us (3%)
  starting transfers between devices  15.2 us (1%)
  between operations  14.7 us (1%)
    reduce_scatter x4, waiting for transfers between devices, normal_map(): lax.psum_scatter(partial_sum, 'views', scatter_dimension=1, tiled=True)  280 us
    all_gather x4, waiting for transfers between devices, normal_map(): gathered = lax.all_gather(vector, 'views', axis=1, tiled=True)  208 us
    dot_general x4, matrix products, forward(): jnp.einsum('crtv,rtkv->crk', columns, projector_tiles, precision=exact_mode)  92.2 us
    psum x3, blocking collectives, norm_total(): return lax.psum(jnp.sum(jnp.square(vector), axis=1), 'views')  87.9 us
    psum x2, blocking collectives, local(): curvature = lax.psum(jnp.sum(direction * mapped, axis=1), 'views')  62.2 us
    scatter-add x4, other arithmetic, backward(): block_grid.at[:, tile_blocks.reshape(-1)]  61.9 us
    dot_general x4, matrix products, backward(): jnp.einsum('crk,rtkv->crtv', ray_parts, projector_tiles, precision=exact_...  60.3 us
    another operation x4, other arithmetic, shrink_patches(): factor = jnp.linalg.cholesky(shifted)  47.1 us
  transfers between devices with their start and end apart: 9, of which 9 were waited for; matrix products, arithmetic and copies ran while one was open for 0% of the time, Pallas kernels for 0%

commit v1 on v0

--- a/solution.py
+++ b/solution.py
@@ -8,6 +8,28 @@
 PENALTY = 1.0
 SHRINK = 16.0
 exact_mode = lax.Precision.HIGHEST
+
+
+def laid_out(blocks, dim):
+    blocks = jnp.moveaxis(blocks, 0, dim)
+    shape = blocks.shape
+    return blocks.reshape(*shape[:dim], shape[dim] * shape[dim + 1], *shape[dim + 2 :])
+
+
+def gather_around(x, axis, dim):
+    count = lax.axis_size(axis)
+    pairs = [(i, (i + 1) % count) for i in range(count)]
+    back = [(b, a) for a, b in pairs]
+    lower, upper = ([], [])
+    for step in range(count - 1):
+        if step % 2 == 0:
+            lower.append(lax.ppermute(lower[-1] if lower else x, axis, pairs))
+        else:
+            upper.append(lax.ppermute(upper[-1] if upper else x, axis, back))
+    parts = jnp.stack([*lower[::-1], x, *upper])
+    shift = lax.axis_index(axis) - len(lower)
+    parts = parts[(jnp.arange(count) - shift) % count]
+    return laid_out(parts, dim)
 
 
 def forward(gathered, projector_tiles, tile_blocks):
@@ -66,7 +88,7 @@
     volume_now, target = (start_volume, target_shard)
 
     def normal_map(vector, measured, anchor):
-        gathered = lax.all_gather(vector, "views", axis=1, tiled=True)
+        gathered = gather_around(vector, "views", 1)
         weighted = ray_scale * (measured - forward(gathered, projector_tiles, tile_blocks))
         partial_sum = backward(weighted, projector_tiles, tile_blocks, voxel_count)
         summed = lax.psum_scatter(partial_sum, "views", scatter_dimension=1, tiled=True)

time: 1060 us -> 1180 us (1.11)
  starting transfers between devices: 15.2 us -> 161 us
  waiting for transfers between devices: 495 us -> 422 us
  local copies, waits for them, and re-layouts: 27 us -> 77.1 us
    all_gather x4 -> x0, waiting for transfers between devices: 208 us -> none  [normal_map(): gathered = lax.all_gather(vector, 'views', axis=1, tiled=True)]
    ppermute x0 -> x60, starting transfers between devices: none -> 146 us  [the longest x28 140 us: gather_around(): upper.append(lax.ppermute(upper[-1] if upper else x, axis, back))]
    ppermute x0 -> x60, waiting for transfers between devices: none -> 91.1 us  [the longest x32 89.6 us: gather_around(): lower.append(lax.ppermute(lower[-1] if lower else x, axis, pairs))]
    reduce_scatter x4, waiting for transfers between devices: 280 us -> 326 us  [normal_map(): lax.psum_scatter(partial_sum, 'views', scatter_dimension=1, tiled=True)]
    unnamed x33 -> x87, local copies, waits for them, and re-layouts: 12.7 us -> 52.1 us
  transfers between devices with their start and end apart: 9 -> 65, of which waited for: 9 -> 40; matrix products, arithmetic and copies ran while one was open for 0% -> 4% of each run, Pallas kernels for 0% -> 0%
where the time goes in v1:
time: 1180 us
  waiting for transfers between devices  422 us (36%)
  other arithmetic  178 us (15%)
  blocking collectives  169 us (14%)
  starting transfers between devices  161 us (14%)
  matrix products  155 us (13%)
  local copies, waits for them, and re-layouts  77.1 us (7%)
  between operations  14.5 us (1%)
    reduce_scatter x4, waiting for transfers between devices, normal_map(): lax.psum_scatter(partial_sum, 'views', scatter_dimension=1, tiled=True)  326 us
    ppermute x28, starting transfers between devices, gather_around(): upper.append(lax.ppermute(upper[-1] if upper else x, axis, back))  140 us
    dot_general x4, matrix products, forward(): jnp.einsum('crtv,rtkv->crk', columns, projector_tiles, precision=exact_mode)  92.8 us
    ppermute x32, waiting for transfers between devices, gather_around(): lower.append(lax.ppermute(lower[-1] if lower else x, axis, pairs))  89.6 us
    psum x3, blocking collectives, norm_total(): return lax.psum(jnp.sum(jnp.square(vector), axis=1), 'views')  87.9 us
    psum x2, blocking collectives, local(): curvature = lax.psum(jnp.sum(direction * mapped, axis=1), 'views')  62 us
    scatter-add x4, other arithmetic, backward(): block_grid.at[:, tile_blocks.reshape(-1)]  61.9 us
    dot_general x4, matrix products, backward(): jnp.einsum('crk,rtkv->crtv', ray_parts, projector_tiles, precision=exact_...  60.2 us
  transfers between devices with their start and end apart: 65, of which 40 were waited for; matrix products, arithmetic and copies ran while one was open for 4% of the time, Pallas kernels for 0%

profile of v1, /device:TPU:1, one launch (start us, length us, event | category | flops | bytes accessed | tf_op | source)
XLA Modules:
  0.0 1176.5 jit_solution(4232421577170032646)
XLA Ops:
  9.3 7.1 collective-permute-done
  60.5 5.5 collective-permute-start.14
  83.3 24.3 %fusion.16 = f32[8,4,128,1]{2,0,3,1:T(8,128)S(1)} fusion(f32[8,512]{1,0:T(8,128)S(1)} %copy-done.11, f32[8,4,48,256]{3,0,2,1:T(8,128)} %bitcast.339, f32[4,48,128,256]{3,2,1,0:T(8,128)} %param.8, f32[8,512]{1,0:T(8,128)S(1)} %copy-done.9, f32[512]{0:T(512)S(1)} %convert_bitcast_fusion), kind=kOutput, calls=%fused_computation.33 | convolution fusion | flops 603992064 | bytes 26789888 | tf_op jit(solution)/shard_map/crtv,rtkv->crk/dot_general | solution.py:40
  107.7 12.9 %fusion.28 = f32[4,8,48,256]{3,1,2,0:T(8,128)} fusion(f32[8,4,128,1]{2,0,3,1:T(8,128)S(1)} %fusion.16, f32[4,48,128,256]{3,2,1,0:T(8,128)S(1)} %copy-done), kind=kOutput, calls=%fused_computation.142 | convolution fusion | flops 603979776 | bytes 26755072 | tf_op jit(solution)/shard_map/crk,rtkv->crtv/dot_general | solution.py:48
  120.7 15.5 %scatter_fusion = f32[8,256,256]{2,0,1:T(8,128)S(1)} fusion(f32[8,256,256]{2,0,1:T(8,128)S(1)} %broadcast.210.clone, s32[192]{0:T(256)S(1)} %bitcast.344, f32[192,8,256]{2,1,0:T(8,128)} %bitcast.333), kind=kCustom, calls=%fused_computation.8 | custom fusion | flops 393216 | bytes 4719360 | tf_op jit(solution)/shard_map/scatter-add | solution.py:50
  137.8 19.4 %all_to_all.33 = f32[1,64,512]{2,0,1:T(1,128)S(1)} all-to-all(f32[1,64,512]{2,0,1:T(1,128)S(1)} %copy.91), channel_id=1, replica_groups=mesh['energy'=8,'views'=16] {'energy'}, dimensions={1} | all-to-all | bytes 262144 | tf_op jit(solution)/shard_map/all_to_all | solution.py:83
  157.2 58.7 %reduce-scatter.5.cloned.1.call-done = f32[8,4096]{1,0:T(8,128)} async-done(((f32[8,65536]{1,0:T(8,128)}), f32[8,4096]{1,0:T(8,128)}) %reduce-scatter.5.cloned.1.call-update) | async-done | bytes 131088 | tf_op jit(solution)/shard_map/reduce_scatter | solution.py:94
  217.4 6.6 collective-permute-done.15
  291.9 22.8 %fusion.13 = f32[8,4,128,1]{2,0,3,1:T(8,128)S(1)} fusion(f32[8,4,48,256]{3,0,2,1:T(8,128)} %bitcast.337, f32[4,48,128,256]{3,2,1,0:T(8,128)} %param.8, f32[8,512]{1,0:T(8,128)S(1)} %copy-done.9, f32[512]{0:T(512)S(1)} %convert_bitcast_fusion), kind=kOutput, calls=%fused_computation.29 | convolution fusion | flops 603992064 | bytes 26773504 | tf_op jit(solution)/shard_map/crtv,rtkv->crk/dot_general | solution.py:40
  314.7 15.7 %fusion.29 = f32[4,8,48,256]{3,1,2,0:T(8,128)} fusion(f32[8,4,128,1]{2,0,3,1:T(8,128)S(1)} %fusion.13, f32[4,48,128,256]{3,2,1,0:T(8,128)} %param.8), kind=kOutput, calls=%fused_computation.143 | convolution fusion | flops 603979776 | bytes 26755072 | tf_op jit(solution)/shard_map/crk,rtkv->crtv/dot_general | solution.py:48
  330.6 15.5 %scatter_fusion.1 = f32[8,256,256]{2,0,1:T(8,128)S(1)} fusion(f32[8,256,256]{2,0,1:T(8,128)S(1)} %broadcast.210.clone.1, s32[192]{0:T(256)S(1)} %bitcast.345, f32[192,8,256]{2,1,0:T(8,128)} %bitcast.334), kind=kCustom, calls=%fused_computation.9 | custom fusion | flops 393216 | bytes 4719360 | tf_op jit(solution)/shard_map/scatter-add | solution.py:50
  347.5 79.3 %reduce-scatter.7.cloned.1.call-done = f32[8,4096]{1,0:T(8,128)} async-done(((f32[8,65536]{1,0:T(8,128)}), f32[8,4096]{1,0:T(8,128)}) %reduce-scatter.7.cloned.1.call-update) | async-done | bytes 131088 | tf_op jit(solution)/shard_map/reduce_scatter | solution.py:94
  427.9 30.9 %all-reduce = (f32[8]{0:T(128)S(1)}, f32[8]{0:T(128)S(1)}) all-reduce(f32[8]{0:T(128)S(1)} %get-tuple-element.7, f32[8]{0:T(128)S(1)} %get-tuple-element.6), channel_id=1, replica_groups=mesh['energy'=8,'views'=16] {'views'}, use_global_device_ids=true, to_apply=%region_3.4 | all-reduce | flops 16 | bytes 128 | tf_op jit(solution)/shard_map/psum | solution.py:100
  459.9 28.5 %psum.44 = f32[8]{0:T(128)S(1)} all-reduce(f32[8]{0:T(128)S(1)} %get-tuple-element.10), channel_id=1, replica_groups=mesh['energy'=8,'views'=16] {'views'}, use_global_device_ids=true, to_apply=%region_9.10 | all-reduce | flops 8 | bytes 64 | tf_op jit(solution)/shard_map/psum | solution.py:100
  490.2 5.9 collective-permute-done.30
  539.1 5.5 collective-permute-start.44
  562.6 22.8 %fusion.9 = f32[8,4,128,1]{2,0,3,1:T(8,128)S(1)} fusion(f32[8,4,48,256]{3,0,2,1:T(8,128)} %bitcast.338, f32[4,48,128,256]{3,2,1,0:T(8,128)} %param.8, f32[8,512]{1,0:T(8,128)S(1)} %copy-done.9, f32[512]{0:T(512)S(1)} %convert_bitcast_fusion), kind=kOutput, calls=%fused_computation.24 | convolution fusion | flops 603992064 | bytes 26773504 | tf_op jit(solution)/shard_map/crtv,rtkv->crk/dot_general | solution.py:40
  585.4 15.7 %fusion.30 = f32[4,8,48,256]{3,1,2,0:T(8,128)} fusion(f32[8,4,128,1]{2,0,3,1:T(8,128)S(1)} %fusion.9, f32[4,48,128,256]{3,2,1,0:T(8,128)} %param.8), kind=kOutput, calls=%fused_computation.144 | convolution fusion | flops 603979776 | bytes 26755072 | tf_op jit(solution)/shard_map/crk,rtkv->crtv/dot_general | solution.py:48
  601.3 15.5 %scatter_fusion.2 = f32[8,256,256]{2,0,1:T(8,128)S(1)} fusion(f32[8,256,256]{2,0,1:T(8,128)S(1)} %broadcast.210.clone.2, s32[192]{0:T(256)S(1)} %bitcast.346, f32[192,8,256]{2,1,0:T(8,128)} %bitcast.335), kind=kCustom, calls=%fused_computation.10 | custom fusion | flops 393216 | bytes 4719360 | tf_op jit(solution)/shard_map/scatter-add | solution.py:50
  618.1 93.6 %reduce-scatter.9.cloned.1.call-done = f32[8,4096]{1,0:T(8,128)} async-done(((f32[8,65536]{1,0:T(8,128)}), f32[8,4096]{1,0:T(8,128)}) %reduce-scatter.9.cloned.1.call-update) | async-done | bytes 131088 | tf_op jit(solution)/shard_map/reduce_scatter | solution.py:94
  712.8 30.9 %psum.45 = f32[8]{0:T(128)S(1)} all-reduce(f32[8]{0:T(128)S(1)} %multiply_reduce_fusion.2), channel_id=1, replica_groups=mesh['energy'=8,'views'=16] {'views'}, use_global_device_ids=true, to_apply=%region_13.14 | all-reduce | flops 8 | bytes 64 | tf_op jit(solution)/shard_map/psum | solution.py:106
  744.8 28.5 %psum.46 = f32[8]{0:T(128)S(1)} all-reduce(f32[8]{0:T(128)S(1)} %multiply_reduce_fusion.1), channel_id=1, replica_groups=mesh['energy'=8,'views'=16] {'views'}, use_global_device_ids=true, to_apply=%region_15.16 | all-reduce | flops 8 | bytes 64 | tf_op jit(solution)/shard_map/psum | solution.py:100
  776.0 5.6 collective-permute-done.45
  848.4 22.8 %fusion.5 = f32[8,4,128,1]{2,0,3,1:T(8,128)S(1)} fusion(f32[8,4,48,256]{3,0,2,1:T(8,128)} %bitcast.336, f32[4,48,128,256]{3,2,1,0:T(8,128)} %param.8, f32[8,512]{1,0:T(8,128)S(1)} %copy-done.9, f32[512]{0:T(512)S(1)} %convert_bitcast_fusion), kind=kOutput, calls=%fused_computation.19 | convolution fusion | flops 603992064 | bytes 26773504 | tf_op jit(solution)/shard_map/crtv,rtkv->crk/dot_general | solution.py:40
  871.2 15.7 %fusion.31 = f32[4,8,48,256]{3,1,2,0:T(8,128)} fusion(f32[8,4,128,1]{2,0,3,1:T(8,128)S(1)} %fusion.5, f32[4,48,128,256]{3,2,1,0:T(8,128)} %param.8), kind=kOutput, calls=%fused_computation.145 | convolution fusion | flops 603979776 | bytes 26755072 | tf_op jit(solution)/shard_map/crk,rtkv->crtv/dot_general | solution.py:48
  887.1 15.5 %scatter_fusion.3 = f32[8,256,256]{2,0,1:T(8,128)S(1)} fusion(f32[8,256,256]{2,0,1:T(8,128)S(1)} %broadcast.210, s32[192]{0:T(256)S(1)} %bitcast.347, f32[192,8,256]{2,1,0:T(8,128)} %bitcast.332), kind=kCustom, calls=%fused_computation.11 | custom fusion | flops 393216 | bytes 4719360 | tf_op jit(solution)/shard_map/scatter-add | solution.py:50
  904.0 93.9 %reduce-scatter.11.cloned.1.call-done = f32[8,4096]{1,0:T(8,128)} async-done(((f32[8,65536]{1,0:T(8,128)}), f32[8,4096]{1,0:T(8,128)}) %reduce-scatter.11.cloned.1.call-update) | async-done | bytes 131088 | tf_op jit(solution)/shard_map/reduce_scatter | solution.py:94
  998.9 31.1 %psum.47 = f32[8]{0:T(128)S(1)} all-reduce(f32[8]{0:T(128)S(1)} %multiply_reduce_fusion), channel_id=1, replica_groups=mesh['energy'=8,'views'=16] {'views'}, use_global_device_ids=true, to_apply=%region_19.20 | all-reduce | flops 8 | bytes 64 | tf_op jit(solution)/shard_map/psum | solution.py:106
  1033.1 19.4 %reduce.6 = f32[4096,8]{1,0:T(8,128)} reduce(f32[4096,1,8]{2,1,0:T(1,128)S(1)} %bitcast.326, f32[]{:T(128)} %broadcast.259), dimensions={1}, to_apply=%bitcast.303.reduce_sub_computation | reduce | bytes 262148
  1055.8 14.3 %all-to-all-start.1 = ((f32[8,1,4096]{2,1,0:T(1,128)}), f32[8,1,4096]{2,1,0:T(1,128)S(1)}, u32[]{:S(2)}, u32[]{:S(2)}) async-start(f32[8,1,4096]{2,1,0:T(1,128)} %reshape.319), calls=%async_computation.5 | async-start | bytes 262144 | tf_op jit(solution)/shard_map/all_to_all | solution.py:114
  1081.2 46.9 %custom-call.11 = f32[8,64,64]{2,1,0:T(8,128)S(1)} custom-call(f32[8,64,64]{2,1,0:T(8,128)S(1)} %fusion.21), custom_call_target="Cholesky" | custom-call | tf_op jit(solution)/shard_map/jit(cholesky)/cholesky | solution.py:61
  1128.4 39.3 %custom-call.12 = f32[8,1,64,64]{2,3,1,0:T(8,128)S(1)} custom-call(f32[8,1,64,64]{3,2,1,0:T(8,128)S(1)} %select_bitcast_fusion), custom_call_target="InvertDiagBlocksLowerTriangular" | custom-call | tf_op jit(solution)/shard_map/jit(_cho_solve)/vmap()/triangular_solve | solution.py:63
  (270 shorter events, 296.4 us)
Async XLA Ops:
  7.2 208.7 %reduce-scatter.5.cloned.1.call-start = ((), (), s32[]{:S(2)}) async-start(), calls=%async_computation.6 | async-start | bytes 2228224 | tf_op jit(solution)/shard_map/reduce_scatter | solution.py:94
  7.2 9.2 collective-permute-start
  23.6 7.9 collective-permute-start.9
  52.1 7.7 collective-permute-start.6
  52.5 8.0 collective-permute-start.13
  59.9 8.5 collective-permute-start.7
  60.5 17.8 %collective-permute-start.14 = (f32[8,4096]{1,0:T(8,128)S(1)}, f32[8,4096]{1,0:T(8,128)S(1)}, u32[]{:S(2)}, u32[]{:S(2)}) collective-permute-start(f32[8,4096]{1,0:T(8,128)S(1)} %collective-permute-done.13), channel_id=1, source_target_pairs={{1,0},{2,1},{3,2},{4,3},{5,4},{6,5},{7,6},{8,7},{9,8},{10,9},{11,1... | collective-permute-start | bytes 393224 | tf_op jit(solution)/shard_map/ppermute | solution.py:28
  137.6 289.3 %reduce-scatter.7.cloned.1.call-start = ((), (), s32[]{:S(2)}) async-start(), calls=%async_computation.7 | async-start | bytes 2228224 | tf_op jit(solution)/shard_map/reduce_scatter | solution.py:94
  216.8 7.2 collective-permute-start.15
  224.1 7.7 collective-permute-start.23
  231.2 7.6 collective-permute-start.17
  246.0 7.6 collective-permute-start.19
  246.0 7.6 collective-permute-start.26
  253.6 8.6 collective-permute-start.20
  253.6 8.6 collective-permute-start.27
  262.2 7.7 collective-permute-start.21
  262.2 7.7 collective-permute-start.28
  269.9 17.0 %collective-permute-start.29 = (f32[8,4096]{1,0:T(8,128)S(1)}, f32[8,4096]{1,0:T(8,128)S(1)}, u32[]{:S(2)}, u32[]{:S(2)}) collective-permute-start(f32[8,4096]{1,0:T(8,128)S(1)} %collective-permute-done.28), channel_id=1, source_target_pairs={{1,0},{2,1},{3,2},{4,3},{5,4},{6,5},{7,6},{8,7},{9,8},{10,9},{11,1... | collective-permute-start | bytes 393224 | tf_op jit(solution)/shard_map/ppermute | solution.py:28
  347.4 364.3 %reduce-scatter.9.cloned.1.call-start = ((), (), s32[]{:S(2)}) async-start(), calls=%async_computation.8 | async-start | bytes 2228224 | tf_op jit(solution)/shard_map/reduce_scatter | solution.py:94
  488.5 7.5 collective-permute-start.30
  496.0 7.2 collective-permute-start.38
  531.8 7.3 collective-permute-start.36
  531.8 7.3 collective-permute-start.43
  539.1 8.6 collective-permute-start.37
  539.1 18.4 %collective-permute-start.44 = (f32[8,4096]{1,0:T(8,128)S(1)}, f32[8,4096]{1,0:T(8,128)S(1)}, u32[]{:S(2)}, u32[]{:S(2)}) collective-permute-start(f32[8,4096]{1,0:T(8,128)S(1)} %collective-permute-done.43), channel_id=1, source_target_pairs={{1,0},{2,1},{3,2},{4,3},{5,4},{6,5},{7,6},{8,7},{9,8},{10,9},{11,1... | collective-permute-start | bytes 393224 | tf_op jit(solution)/shard_map/ppermute | solution.py:28
  618.1 379.7 %reduce-scatter.11.cloned.1.call-start = ((), (), s32[]{:S(2)}) async-start(), calls=%async_computation.9 | async-start | bytes 2228224 | tf_op jit(solution)/shard_map/reduce_scatter | solution.py:94
  774.4 7.3 collective-permute-start.45
  817.3 7.5 collective-permute-start.51
  817.4 7.8 collective-permute-start.58
  824.9 8.7 collective-permute-start.52
  825.1 18.3 %collective-permute-start.59 = (f32[8,4096]{1,0:T(8,128)S(1)}, f32[8,4096]{1,0:T(8,128)S(1)}, u32[]{:S(2)}, u32[]{:S(2)}) collective-permute-start(f32[8,4096]{1,0:T(8,128)S(1)} %collective-permute-done.58), channel_id=1, source_target_pairs={{1,0},{2,1},{3,2},{4,3},{5,4},{6,5},{7,6},{8,7},{9,8},{10,9},{11,1... | collective-permute-start | bytes 393224 | tf_op jit(solution)/shard_map/ppermute | solution.py:28
  1055.8 19.5 %all-to-all-start.1 = ((f32[8,1,4096]{2,1,0:T(1,128)}), f32[8,1,4096]{2,1,0:T(1,128)S(1)}, u32[]{:S(2)}, u32[]{:S(2)}) async-start(f32[8,1,4096]{2,1,0:T(1,128)} %reshape.319), calls=%async_computation.5 | async-start | bytes 262144 | tf_op jit(solution)/shard_map/all_to_all | solution.py:114
  (45 other events, 361.6 us)
Sparse Core Ops, SparseCore 0:
  137.7 78.1 reduce-scatter.4
  347.6 79.2 reduce-scatter.6
  618.2 93.5 reduce-scatter.8
  904.1 93.7 reduce-scatter.10
